TPU v7x, 512 devices: a whole 4x4x16 slice. The times are simulated.
512 devices in a mesh: gx: 16 (over x_hi, y, core), gy: 32 (over x_lo, z).
Axes of the slice: x: 4 (x_hi: 2, x_lo: 2; x = x_hi * 2 + x_lo), y: 4, z: 16, core: 2. Of those that a mesh axis runs over, the one named last changes fastest.
Arguments:
- matrix: bfloat16 [2097152, 256], P(('gx', 'gy')), as said below
- pattern: int32 [16384, 2], P(('gx', 'gy')), may hold values 0 or 1
Outputs:
- basis: bfloat16 [2097152, 256], P(('gx', 'gy'))
- upper: float32 [256, 256], replicated
Inputs may be any that keep to these rules, and one draw needn't show every extreme that they name: matrix has full column rank after masking, with columns of unlike scales.
All inputs are finite; a program needn't handle non-finite values. No bound on the sum of `pattern` on one device may be relied on, other than what follows from the above.
Results may differ from a plain program's by a relative error of at most 0.001.
Values sent between devices are 32-bit elements; how exact they have to be, the bound alone decides.
A program may use at most 64 MiB of HBM per device.

v0:
```python
import jax
import jax.numpy as jnp
from jax import lax
from jax.sharding import PartitionSpec as P

BLOCK = 128


def factor_gram(gram):
    count = gram.shape[0]
    column_ids = jnp.arange(count, dtype=jnp.int32)

    def one_pivot(step, carry):
        remain, upper = carry
        index = jnp.asarray(step).astype(jnp.int32)
        row = lax.dynamic_slice_in_dim(remain, index, 1, 0)[0]
        pivot = lax.dynamic_slice_in_dim(row, index, 1, 0)[0]
        row = jnp.where(column_ids >= index, row / jnp.sqrt(pivot), jnp.zeros_like(row))
        upper = lax.dynamic_update_slice_in_dim(upper, row[None, :], index, 0)
        remain = remain - row[:, None] * row[None, :]
        return (remain, upper)

    _, upper = lax.fori_loop(0, count, one_pivot, (gram, jnp.zeros_like(gram)))
    return upper


def invert_upper(upper):
    count = upper.shape[0]
    column_ids = jnp.arange(count, dtype=jnp.int32)

    def one_row(step, inverse):
        index = (count - 1 - jnp.asarray(step)).astype(jnp.int32)
        row = lax.dynamic_slice_in_dim(upper, index, 1, 0)[0]
        pivot = lax.dynamic_slice_in_dim(row, index, 1, 0)[0]
        unit = (column_ids == index).astype(upper.dtype)
        solved = (unit - jnp.dot(row, inverse, precision=lax.Precision.HIGHEST)) / pivot
        return lax.dynamic_update_slice_in_dim(inverse, solved[None, :], index, 0)

    return lax.fori_loop(0, count, one_row, jnp.zeros_like(upper))


def local(matrix, pattern):
    rows, width = matrix.shape
    keep = pattern.astype(jnp.bfloat16)
    blocks = matrix.reshape(rows // BLOCK, BLOCK, width // BLOCK, BLOCK)
    masked = (blocks * keep[:, None, :, None]).reshape(rows, width)
    total_rows = rows * lax.axis_size("gx") * lax.axis_size("gy")
    gram = lax.dot_general(
        masked, masked, (((0,), (0,)), ((), ())), preferred_element_type=jnp.float32
    )
    gram = lax.psum(gram, ("gx", "gy"))
    gram = gram / jnp.float32(total_rows)
    upper = factor_gram(gram)
    inverse = invert_upper(upper)
    basis = jnp.dot(masked.astype(jnp.float32), inverse, precision=lax.Precision.HIGHEST).astype(
        jnp.bfloat16
    )
    return (basis, upper)


def solution(mesh):
    placed = (P(("gx", "gy"), None), P(("gx", "gy"), None))
    return jax.shard_map(
        local, mesh=mesh, in_specs=placed, out_specs=(P(("gx", "gy"), None), P()), check_vma=False
    )
```

profile of v0, /device:TPU:1, one launch (start us, length us, event | category | flops | bytes accessed | tf_op | source)
XLA Modules:
  0.0 1272.0 jit_solution(5966582722841789088)
XLA Ops:
  8.0 1.1 mul.67
  9.6 1.5 fusion.10
  11.1 464.2 %all-reduce.2.cloned.1.call-done = f32[256,256]{1,0:T(8,128)} async-done(((f32[256,256]{1,0:T(8,128)}), f32[256,256]{1,0:T(8,128)}) %all-reduce.2.cloned.1.call-update) | async-done | bytes 262160 | tf_op jit(solution)/shard_map/psum | solution.py:51
  475.3 1.0 broadcast_multiply_fusion
  476.3 387.9 %while.36 = (s32[]{:T(128)}, f32[256,256]{1,0:T(8,128)S(1)}, f32[256,256]{1,0:T(8,128)S(1)}, s32[]{:T(128)}, s32[]{:T(128)}, /*index=5*/s32[]{:T(128)}) while((s32[]{:T(128)}, f32[256,256]{1,0:T(8,128)S(1)}, f32[256,256]{1,0:T(8,128)S(1)}, s32[]{:T(128)}, s32[]{:T(128)}, /*index=5*/s32[]{:T(128)}) %tuple.86), condition=%wide.region_2.3_spmd.clone, body=%wide.region_1.2_spmd.clone.sunk | while | flops 132355 | bytes 534149 | solution.py:23
  864.2 396.1 %while.37 = (s32[]{:T(128)}, f32[256,256]{1,0:T(8,128)S(1)}, f32[256,256]{1,0:T(8,128)S(1)}, s32[]{:T(128)}, s32[]{:T(128)}, /*index=5*/s32[]{:T(128)}, s32[]{:T(128)}) while((s32[]{:T(128)}, f32[256,256]{1,0:T(8,128)S(1)}, f32[256,256]{1,0:T(8,128)S(1)}, s32[]{:T(128)}, s32[]{:T(128)}, /*index=5*/s32[]{:T(128)}, s32[]{:T(128)}) %tuple.89), condition=%wide.region_4.5_spmd.clone, body=%wide.region_3.4_spmd.clone.sunk | while | flops 787463 | bytes 268463 | solution.py:39
  868.1 0.7 fusion.20
  871.2 0.7 fusion.20
  874.3 0.7 fusion.20
  875.8 0.7 fusion.20
  878.9 0.7 fusion.20
  882.0 0.7 fusion.20
  885.1 0.7 fusion.20
  886.7 0.7 fusion.20
  889.8 0.7 fusion.20
  892.9 0.7 fusion.20
  897.5 0.7 fusion.20
  900.6 0.7 fusion.20
  903.7 0.7 fusion.20
  905.2 0.7 fusion.20
  908.3 0.7 fusion.20
  911.4 0.7 fusion.20
  914.5 0.7 fusion.20
  916.1 0.7 fusion.20
  919.2 0.7 fusion.20
  922.3 0.7 fusion.20
  926.9 0.7 fusion.20
  930.0 0.7 fusion.20
  933.1 0.7 fusion.20
  934.6 0.7 fusion.20
  937.7 0.7 fusion.20
  1260.4 4.8 convolution_convert_fusion
  (2545 shorter events, 567.2 us)
Async XLA Ops:
  7.2 468.1 %all-reduce.2.cloned.1.call-start = ((), (), s32[]{:S(2)}) async-start(), calls=%async_computation | async-start | bytes 524288 | tf_op jit(solution)/shard_map/psum | solution.py:51
  8.0 1.6 copy-start
  1260.3 4.9 copy-start.1
Sparse Core Ops, SparseCore 0:
  14.0 461.2 all-reduce.1
where the time goes:
time: 1290 us; the launch traced here: 1270 us
  waiting for transfers between devices  464 us (36%)
  local copies, waits for them, and re-layouts  326 us (25%)
  other arithmetic  214 us (17%)
  loops' own time  201 us (16%)
  matrix products  53.1 us (4%)
  between operations  14.1 us (1%)
    psum x1, waiting for transfers between devices, local(): gram = lax.psum(gram, ('gx', 'gy'))  464 us
    another operation x1, loops' own time, factor_gram(): _, upper = lax.fori_loop(0, count, one_pivot, (gram, jnp.zeros_like(gram)))  191 us
    div x256, other arithmetic, one_row(): (unit - jnp.dot(row, inverse, precision=lax.Precision.HIGHEST)) / pivot  178 us
    dynamic_slice x256, local copies, waits for them, and re-layouts, one_pivot(): pivot = lax.dynamic_slice_in_dim(row, index, 1, 0)[0]  151 us
    dynamic_slice x256, local copies, waits for them, and re-layouts, one_row(): pivot = lax.dynamic_slice_in_dim(row, index, 1, 0)[0]  151 us
    dot_general x256, matrix products, one_row(): jnp.dot(row, inverse, precision=lax.Precision.HIGHEST)  46.8 us
    sub x256, other arithmetic, one_pivot(): remain = remain - row[:, None] * row[None, :]  28.7 us
  transfers between devices with their start and end apart: 1, of which 1 were waited for; matrix products, arithmetic and copies ran while one was open for 0% of the time, Pallas kernels for 0%

commit v1 on v0

v1 whole, which is shorter than its diff:
```python
import functools

import jax
import jax.numpy as jnp
from jax import lax
from jax.experimental import pallas as pl
from jax.experimental.pallas import tpu as pltpu
from jax.sharding import PartitionSpec as P

BLOCK = 128
NB = 256
F32 = jnp.float32
BF16 = jnp.bfloat16
HIGHEST = lax.Precision.HIGHEST
MESH = pl.DeviceIdType.MESH

NX, NY, NZ, NC = 4, 4, 16, 2
PLANE = NX * NY * NC
PIECE = 9


def ring(step, size):
    return min(step, size - step)


PLANE_STEPS = sorted(
    ((dx, dy, dc) for dx in range(NX) for dy in range(NY) for dc in range(NC) if dx or dy or dc),
    key=lambda s: -(ring(s[0], NX) + ring(s[1], NY) + 0.5 * s[2]),
)
Z_STEPS = sorted(range(1, NZ), key=lambda s: -ring(s, NZ))


def place():
    gx, gy = lax.axis_index("gx"), lax.axis_index("gy")
    x = gx // (NY * NC) * 2 + gy // NZ
    return x, gx // NC % NY, gy % NZ, gx % NC


def device(x, y, z, core):
    return (x // 2 * NY + y) * NC + core, x % 2 * NZ + z


def gram_kernel(chunks, matrix, pattern, out, held, send, recv, zbuf, final,
                in_sems, rs_send, rs_recv, z_send, z_recv, ag_send, ag_recv):
    rows = held.shape[0]
    step = rows // chunks
    loads = []
    for i in range(chunks):
        part = pl.ds(i * step, step)
        load = pltpu.make_async_copy(matrix.at[part], held.at[part], in_sems.at[i])
        load.start()
        loads.append(load)

    x, y, z, core = place()
    mine = (x * NY + y) * NC + core
    plane = []
    for dx, dy, dc in PLANE_STEPS:
        px, py, pc = (x + dx) % NX, (y + dy) % NY, (core + dc) % NC
        plane.append((device(px, py, z, pc), (px * NY + py) * NC + pc))
    line = [device(x, y, (z + dz) % NZ, core) for dz in Z_STEPS]

    barrier = pltpu.get_barrier_semaphore()
    for where, _ in plane:
        pl.semaphore_signal(barrier, inc=1, device_id=where, device_id_type=MESH)
    for where in line:
        pl.semaphore_signal(barrier, inc=1, device_id=where, device_id_type=MESH)

    gram = jnp.zeros((NB, NB), F32)
    for i in range(chunks):
        loads[i].wait()
        blocks = []
        for b in range(step // BLOCK):
            at = i * step + b * BLOCK
            halves = []
            for h in range(NB // BLOCK):
                keep = pattern[at // BLOCK, h] != 0
                halves.append(jnp.where(keep, held[at : at + BLOCK, h * BLOCK : h * BLOCK + BLOCK], 0).astype(BF16))
            blocks.append(jnp.concatenate(halves, axis=1))
        masked = jnp.concatenate(blocks, axis=0)
        gram += lax.dot_general(masked, masked, (((0,), (0,)), ((), ())), preferred_element_type=F32)

    r = lax.broadcasted_iota(jnp.int32, (BLOCK, BLOCK), 0)
    c = lax.broadcasted_iota(jnp.int32, (BLOCK, BLOCK), 1)
    g00, g01, g11 = gram[:BLOCK, :BLOCK], gram[:BLOCK, BLOCK:], gram[BLOCK:, BLOCK:]
    both = jnp.where(c >= r, g00, g11)
    diagonal = jnp.sum(jnp.where(c == r, g11, 0.0), axis=0, keepdims=True)
    send[: PLANE // 2, :8, :] = g01.reshape(PLANE // 2, 8, BLOCK)
    send[PLANE // 2 :, :8, :] = both.reshape(PLANE // 2, 8, BLOCK)
    send[:, 8:, :] = jnp.broadcast_to(diagonal[None], (PLANE, 1, BLOCK))

    pl.semaphore_wait(barrier, len(plane) + len(line))

    copies = []
    for n, (where, piece) in enumerate(plane):
        copy = pltpu.make_async_remote_copy(
            src_ref=send.at[piece], dst_ref=recv.at[n], send_sem=rs_send.at[n], recv_sem=rs_recv.at[n],
            device_id=where, device_id_type=MESH)
        copy.start()
        copies.append(copy)
    for copy in copies:
        copy.wait_recv()
    total = send[mine]
    for n in range(len(plane)):
        total += recv[n]
    zbuf[z] = total

    zcopies = []
    for n, where in enumerate(line):
        copy = pltpu.make_async_remote_copy(
            src_ref=zbuf.at[z], dst_ref=zbuf.at[z], send_sem=z_send.at[n], recv_sem=z_recv.at[z],
            device_id=where, device_id_type=MESH)
        copy.start()
        zcopies.append(copy)
    for dz in Z_STEPS:
        other = (z + dz) % NZ
        pltpu.make_async_remote_copy(
            src_ref=zbuf.at[other], dst_ref=zbuf.at[other], send_sem=z_send.at[0], recv_sem=z_recv.at[other],
            device_id=line[0], device_id_type=MESH).wait_recv()
    total = zbuf[0]
    for n in range(1, NZ):
        total += zbuf[n]
    final[mine] = total

    acopies = []
    for n, (where, _) in enumerate(plane):
        copy = pltpu.make_async_remote_copy(
            src_ref=final.at[mine], dst_ref=final.at[mine], send_sem=ag_send.at[n], recv_sem=ag_recv.at[mine],
            device_id=where, device_id_type=MESH)
        copy.start()
        acopies.append(copy)
    for where, piece in plane:
        pltpu.make_async_remote_copy(
            src_ref=final.at[piece], dst_ref=final.at[piece], send_sem=ag_send.at[0], recv_sem=ag_recv.at[piece],
            device_id=where, device_id_type=MESH).wait_recv()
    out[...] = final[...]
    for copy in copies + zcopies + acopies:
        copy.wait_send()


def summed_gram(matrix, pattern, chunks=4):
    rows = matrix.shape[0]
    piece = (PIECE, BLOCK)
    dma = pltpu.SemaphoreType.DMA
    return pl.pallas_call(
        functools.partial(gram_kernel, chunks),
        out_shape=jax.ShapeDtypeStruct((PLANE,) + piece, F32),
        in_specs=[pl.BlockSpec(memory_space=pl.ANY), pl.BlockSpec(memory_space=pltpu.SMEM)],
        out_specs=pl.BlockSpec(memory_space=pltpu.VMEM),
        scratch_shapes=[
            pltpu.VMEM((rows, NB), BF16),
            pltpu.VMEM((PLANE,) + piece, F32),
            pltpu.VMEM((PLANE - 1,) + piece, F32),
            pltpu.VMEM((NZ,) + piece, F32),
            pltpu.VMEM((PLANE,) + piece, F32),
            dma((chunks,)),
            dma((PLANE - 1,)), dma((PLANE - 1,)),
            dma((NZ - 1,)), dma((NZ,)),
            dma((PLANE - 1,)), dma((PLANE,)),
        ],
        compiler_params=pltpu.CompilerParams(collective_id=0, has_side_effects=True, vmem_limit_bytes=24 << 20),
        cost_estimate=pl.CostEstimate(flops=2 * rows * NB * NB, bytes_accessed=2 * rows * NB, transcendentals=0),
        name="gram_sum",
    )(matrix, pattern)


def eliminate(panel, block):
    size = block.shape[0]
    tiles, lanes = size // 8, panel.shape[1] // 128
    cols = [jnp.broadcast_to(block[k // 8 * 8 :, k : k + 1], (size - k // 8 * 8, 128)) for k in range(size)]
    parts = [[panel[8 * t : 8 * t + 8, 128 * c : 128 * c + 128] for c in range(lanes)] for t in range(tiles)]
    sub = lax.broadcasted_iota(jnp.int32, (8, 128), 0)
    pivots = []
    for j in range(size):
        t0, s = j // 8, j % 8
        col = cols[j]
        pivot = jnp.broadcast_to(col[s : s + 1], (8, 128))
        inverse = 1.0 / pivot
        seen = pivot if s == 0 else jnp.where(sub >= s, pivot, seen)
        if s == 7:
            pivots.append(seen)
        for k in range(j + 1, size):
            first = k // 8 - t0
            row = col[k - 8 * t0 : k - 8 * t0 + 1] * inverse[0:1]
            cols[k] = cols[k] - col[8 * first :] * jnp.broadcast_to(row, (size - k // 8 * 8, 128))
        for t in range(t0, tiles):
            scaled = col[8 * (t - t0) : 8 * (t - t0) + 8] * inverse
            if t == t0:
                if s == 7:
                    continue
                scaled = jnp.where(sub > s, scaled, 0.0)
            for c in range(lanes):
                parts[t][c] = parts[t][c] - scaled * jnp.broadcast_to(parts[t0][c][s : s + 1], (8, 128))
    rows = []
    for t in range(tiles):
        scale = lax.rsqrt(pivots[t])
        rows.append(jnp.concatenate([p * scale for p in parts[t]], axis=1))
    return jnp.concatenate(rows, axis=0)


def factor(work, size):
    n = work.shape[0]
    for r0 in range(0, n, size):
        r1 = r0 + size
        low, high = r0 // 128 * 128, n + (r1 + 127) // 128 * 128
        panel = work[r0:r1, low:high]
        rows = eliminate(panel, panel[:, r0 - low : r1 - low])
        work[r0:r1, low:high] = rows
        cut = r1 // 128 * 128
        for a, e in ((r1, r1 + size), (r1 + size, n)):
            if a < e <= n:
                work[a:e, cut:high] = work[a:e, cut:high] - lax.dot_general(
                    rows[:, a - low : e - low], rows[:, cut - low :], (((0,), (0,)), ((), ())),
                    precision=HIGHEST, preferred_element_type=F32)


def basis_kernel(chunks, total_rows, gram, matrix, pattern, basis, upper, work, held, made, in_sems, out_sems):
    rows = held.shape[0]
    step = rows // chunks
    loads = []
    for i in range(chunks):
        part = pl.ds(i * step, step)
        load = pltpu.make_async_copy(matrix.at[part], held.at[part], in_sems.at[i])
        load.start()
        loads.append(load)

    scale = 1.0 / total_rows
    g01 = gram[: PLANE // 2, :8, :].reshape(BLOCK, BLOCK) * scale
    both = gram[PLANE // 2 :, :8, :].reshape(BLOCK, BLOCK) * scale
    diagonal = gram[0, 8:, :] * scale
    flipped = both.T
    r = lax.broadcasted_iota(jnp.int32, (BLOCK, BLOCK), 0)
    c = lax.broadcasted_iota(jnp.int32, (BLOCK, BLOCK), 1)
    unit = jnp.where(r == c, 1.0, 0.0)
    zero = jnp.zeros((BLOCK, BLOCK), F32)
    work[:BLOCK, :BLOCK] = jnp.where(c >= r, both, flipped)
    work[:BLOCK, BLOCK:NB] = g01
    work[BLOCK:, BLOCK:NB] = jnp.where(c < r, both, jnp.where(c > r, flipped, diagonal))
    work[:BLOCK, NB : NB + BLOCK] = unit
    work[:BLOCK, NB + BLOCK :] = zero
    work[BLOCK:, NB : NB + BLOCK] = zero
    work[BLOCK:, NB + BLOCK :] = unit
    factor(work, 32)
    r = lax.broadcasted_iota(jnp.int32, (NB, NB), 0)
    c = lax.broadcasted_iota(jnp.int32, (NB, NB), 1)
    upper[...] = jnp.where(c >= r, work[:, :NB], 0.0)
    inverse = jnp.where(c <= r, work[:, NB:], 0.0)
    head = inverse.astype(BF16)
    tail = (inverse - head.astype(F32)).astype(BF16)

    stores = []
    for i in range(chunks):
        loads[i].wait()
        blocks = []
        for b in range(step // BLOCK):
            at = i * step + b * BLOCK
            halves = []
            for h in range(NB // BLOCK):
                keep = pattern[at // BLOCK, h] != 0
                halves.append(jnp.where(keep, held[at : at + BLOCK, h * BLOCK : h * BLOCK + BLOCK], 0).astype(BF16))
            blocks.append(jnp.concatenate(halves, axis=1))
        masked = jnp.concatenate(blocks, axis=0)
        dims = (((1,), (1,)), ((), ()))
        result = lax.dot_general(masked, head, dims, preferred_element_type=F32)
        result += lax.dot_general(masked, tail, dims, preferred_element_type=F32)
        part = pl.ds(i * step, step)
        made[part, :] = result.astype(BF16)
        store = pltpu.make_async_copy(made.at[part], basis.at[part], out_sems.at[i])
        store.start()
        stores.append(store)
    for store in stores:
        store.wait()


def factor_and_basis(gram, matrix, pattern, total_rows, chunks=8):
    rows = matrix.shape[0]
    vmem = pl.BlockSpec(memory_space=pltpu.VMEM)
    hbm = pl.BlockSpec(memory_space=pl.ANY)
    return pl.pallas_call(
        functools.partial(basis_kernel, chunks, float(total_rows)),
        out_shape=(jax.ShapeDtypeStruct((rows, NB), BF16), jax.ShapeDtypeStruct((NB, NB), F32)),
        in_specs=[vmem, hbm, pl.BlockSpec(memory_space=pltpu.SMEM)],
        out_specs=(hbm, vmem),
        scratch_shapes=[
            pltpu.VMEM((NB, 2 * NB), F32),
            pltpu.VMEM((rows, NB), BF16),
            pltpu.VMEM((rows, NB), BF16),
            pltpu.SemaphoreType.DMA((chunks,)),
            pltpu.SemaphoreType.DMA((chunks,)),
        ],
        compiler_params=pltpu.CompilerParams(vmem_limit_bytes=24 << 20),
        cost_estimate=pl.CostEstimate(flops=4 * rows * NB * NB, bytes_accessed=4 * rows * NB, transcendentals=0),
        name="factor_basis",
    )(gram, matrix, pattern)


def local(matrix, pattern):
    total_rows = matrix.shape[0] * lax.axis_size("gx") * lax.axis_size("gy")
    gram = summed_gram(matrix, pattern)
    return factor_and_basis(gram, matrix, pattern, total_rows)


def solution(mesh):
    placed = (P(("gx", "gy"), None), P(("gx", "gy"), None))
    return jax.shard_map(
        local, mesh=mesh, in_specs=placed, out_specs=(P(("gx", "gy"), None), P()), check_vma=False
    )
```

time: 1290 us -> 52.9 us (0.04); the launches traced: 1270 us -> 52.7 us
  waiting for transfers between devices: 464 us -> 0 us
  local copies, waits for them, and re-layouts: 326 us -> 2.35 us
  other arithmetic: 214 us -> 0 us
  loops' own time: 201 us -> 0 us
  matrix products: 53.1 us -> 0 us
  Pallas kernels: 0 us -> 49.7 us
  between operations: 14.1 us -> 0.64 us
    psum x1 -> x0, waiting for transfers between devices: 464 us -> none  [local(): gram = lax.psum(gram, ('gx', 'gy'))]
    dynamic_slice x512 -> x0, local copies, waits for them, and re-layouts: 302 us -> none  [the longest x256 151 us: one_pivot(): pivot = lax.dynamic_slice_in_dim(row, index, 1, 0)[0]]
    another operation x2 -> x0, loops' own time: 201 us -> none  [the longest x1 191 us: factor_gram(): _, upper = lax.fori_loop(0, count, one_pivot, (gram, jnp.zeros_like(gram)))]
    div x257 -> x0, other arithmetic: 179 us -> none  [the longest x256 178 us: one_row(): (unit - jnp.dot(row, inverse, precision=lax.Precision.HIGHEST)) / pivot]
    dot_general x258 -> x0, matrix products: 53.1 us -> none  [the longest x256 46.8 us: one_row(): jnp.dot(row, inverse, precision=lax.Precision.HIGHEST)]
    pallas_call x0 -> x2, Pallas kernels: none -> 49.7 us  [the longest x1 36.2 us: summed_gram(): pl.pallas_call(functools.partial(gram_kernel, chunks), out_shape=jax.Shap...]
    sub x256 -> x0, other arithmetic: 28.7 us -> none  [one_pivot(): remain = remain - row[:, None] * row[None, :]]
    dynamic_update_slice x512 -> x0, local copies, waits for them, and re-layouts: 21.8 us -> none  [the longest x256 10.9 us: one_row(): return lax.dynamic_update_slice_in_dim(inverse, solved[None, :], index, 0)]
  transfers between devices with their start and end apart: 1 -> 0, of which waited for: 1 -> 0; matrix products, arithmetic and copies ran while one was open for 0% -> 0% of each run, Pallas kernels for 0% -> 0%
where the time goes in v1:
time: 52.9 us; the launch traced here: 52.7 us
  Pallas kernels  49.7 us (94%)
  local copies, waits for them, and re-layouts  2.35 us (4%)
  between operations  0.64 us (1%)
    pallas_call x1, Pallas kernels, summed_gram(): pl.pallas_call(functools.partial(gram_kernel, chunks), out_shape=jax.Shap...  36.2 us
    pallas_call x1, Pallas kernels, factor_and_basis(): pl.pallas_call(functools.partial(basis_kernel, chunks, float(total_rows))...  13.5 us
    unnamed x3, local copies, waits for them, and re-layouts  2.35 us

profile of v1, /device:TPU:1, one launch (start us, length us, event | category | flops | bytes accessed | tf_op | source)
XLA Modules:
  0.0 52.7 jit_solution(4348807156695797195)
XLA Ops:
  0.6 0.8 %copy.4.pattern = s32[32,2]{1,0:T(8,128)S(1)} copy(s32[32,2]{0,1:T(2,128)} %param.3) | data formatting | bytes 512 | tf_op args[1]
  1.4 0.0 copy-start
  1.4 1.6 %copy-done = bf16[4096,256]{1,0:T(8,128)(2,1)S(1)} copy-done((bf16[4096,256]{1,0:T(8,128)(2,1)S(1)}, bf16[4096,256]{1,0:T(8,128)(2,1)}, u32[]{:S(2)}) %copy-start) | copy-done | bytes 2097176
  3.0 36.2 %gram_sum.1.gram = f32[32,9,128]{2,1,0:T(8,128)S(1)} custom-call(bf16[4096,256]{1,0:T(8,128)(2,1)S(1)} %copy-done, s32[32,2]{1,0:T(8,128)S(1)} %copy.4.pattern), custom_call_target="tpu_custom_call" | custom-call | flops 536870912 | bytes 2097152 | tf_op jit(solution)/shard_map/gram_sum/pallas_call | solution.py:144
  39.2 13.5 %factor_basis.1 = (bf16[4096,256]{1,0:T(8,128)(2,1)}, f32[256,256]{1,0:T(8,128)}) custom-call(f32[32,9,128]{2,1,0:T(8,128)S(1)} %gram_sum.1.gram, bf16[4096,256]{1,0:T(8,128)(2,1)S(1)} %copy-done, s32[32,2]{1,0:T(8,128)S(1)} %copy.4.pattern), custom_call_target="tpu_custom_call" | custom-call | flops 1073741824 | bytes 4194304 | tf_op jit(solution)/shard_map/factor_basis/pallas_call | solution.py:278
Async XLA Ops:
  1.4 1.6 %copy-start = (bf16[4096,256]{1,0:T(8,128)(2,1)S(1)}, bf16[4096,256]{1,0:T(8,128)(2,1)}, u32[]{:S(2)}) copy-start(bf16[4096,256]{1,0:T(8,128)(2,1)} %matrix.3) | copy-start | bytes 6291460

commit v2 on v1

v2 whole, which is shorter than its diff:
```python
import functools

import jax
import jax.numpy as jnp
from jax import lax
from jax.experimental import pallas as pl
from jax.experimental.pallas import tpu as pltpu
from jax.sharding import PartitionSpec as P

BLOCK = 128
NB = 256
F32 = jnp.float32
BF16 = jnp.bfloat16
MESH = pl.DeviceIdType.MESH

NX, NY, NZ, NC = 4, 4, 16, 2
PLANE = NX * NY * NC
PIECE = 9


def ring(step, size):
    return min(step, size - step)


PLANE_STEPS = sorted(
    ((dx, dy, dc) for dx in range(NX) for dy in range(NY) for dc in range(NC) if dx or dy or dc),
    key=lambda s: -(ring(s[0], NX) + ring(s[1], NY) + 0.5 * s[2]),
)
Z_STEPS = sorted(range(1, NZ), key=lambda s: -ring(s, NZ))
Z_NEAR = [s for s in Z_STEPS if ring(s, NZ) <= 4]


def place():
    gx, gy = lax.axis_index("gx"), lax.axis_index("gy")
    x = gx // (NY * NC) * 2 + gy // NZ
    return x, gx // NC % NY, gy % NZ, gx % NC


def device(x, y, z, core):
    return (x // 2 * NY + y) * NC + core, x % 2 * NZ + z


def gram_kernel(chunks, matrix, pattern, out, masked, keeps, send, recv, zbuf, final,
                in_sems, keep_sem, rs_send, rs_recv, z_send, z_recv, ag_send, ag_recv, far_sem):
    rows = masked.shape[0]
    step = rows // chunks
    x, y, z, core = place()
    mine = (x * NY + y) * NC + core
    plane = []
    for dx, dy, dc in PLANE_STEPS:
        px, py, pc = (x + dx) % NX, (y + dy) % NY, (core + dc) % NC
        plane.append((device(px, py, z, pc), (px * NY + py) * NC + pc))
    line = {dz: device(x, y, (z + dz) % NZ, core) for dz in Z_STEPS}

    barrier = pltpu.get_barrier_semaphore()
    for where, _ in plane:
        pl.semaphore_signal(barrier, inc=1, device_id=where, device_id_type=MESH)
    for dz in Z_NEAR:
        pl.semaphore_signal(barrier, inc=1, device_id=line[dz], device_id_type=MESH)

    keep_load = pltpu.make_async_copy(pattern, keeps, keep_sem)
    keep_load.start()
    loads = []
    for i in range(chunks):
        part = pl.ds(i * step, step)
        load = pltpu.make_async_copy(matrix.at[part], masked.at[part], in_sems.at[i])
        load.start()
        loads.append(load)

    keep_load.wait()
    gram = jnp.zeros((NB, NB), F32)
    for i in range(chunks):
        loads[i].wait()
        for at in range(i * step, i * step + step, BLOCK):
            for h in range(NB // BLOCK):
                block = (slice(at, at + BLOCK), slice(h * BLOCK, h * BLOCK + BLOCK))
                masked[block] = jnp.where(keeps[h, at // BLOCK] != 0, masked[block], 0).astype(BF16)
        part = masked[i * step : i * step + step, :]
        gram += lax.dot_general(part, part, (((0,), (0,)), ((), ())), preferred_element_type=F32)

    r = lax.broadcasted_iota(jnp.int32, (BLOCK, BLOCK), 0)
    c = lax.broadcasted_iota(jnp.int32, (BLOCK, BLOCK), 1)
    g00, g01, g11 = gram[:BLOCK, :BLOCK], gram[:BLOCK, BLOCK:], gram[BLOCK:, BLOCK:]
    both = jnp.where(c >= r, g00, g11)
    diagonal = jnp.sum(jnp.where(c == r, g11, 0.0), axis=0, keepdims=True)
    send[: PLANE // 2, :8, :] = g01.reshape(PLANE // 2, 8, BLOCK)
    send[PLANE // 2 :, :8, :] = both.reshape(PLANE // 2, 8, BLOCK)
    send[:, 8:, :] = jnp.broadcast_to(diagonal[None], (PLANE, 1, BLOCK))

    pl.semaphore_wait(barrier, len(plane) + len(Z_NEAR))

    copies = []
    for n, (where, piece) in enumerate(plane):
        copy = pltpu.make_async_remote_copy(
            src_ref=send.at[piece], dst_ref=recv.at[n], send_sem=rs_send.at[n], recv_sem=rs_recv.at[n],
            device_id=where, device_id_type=MESH)
        copy.start()
        copies.append(copy)
    for dz in (4, NZ - 4):
        pl.semaphore_signal(far_sem, inc=1, device_id=line[dz], device_id_type=MESH)
    for copy in copies:
        copy.wait_recv()
    total = send[mine]
    for n in range(len(plane)):
        total += recv[n]
    zbuf[z] = total
    pl.semaphore_wait(far_sem, 2)

    zcopies = []
    for n, dz in enumerate(Z_STEPS):
        copy = pltpu.make_async_remote_copy(
            src_ref=zbuf.at[z], dst_ref=zbuf.at[z], send_sem=z_send.at[n], recv_sem=z_recv.at[z],
            device_id=line[dz], device_id_type=MESH)
        copy.start()
        zcopies.append(copy)
    for dz in Z_STEPS:
        other = (z + dz) % NZ
        pltpu.make_async_remote_copy(
            src_ref=zbuf.at[other], dst_ref=zbuf.at[other], send_sem=z_send.at[0], recv_sem=z_recv.at[other],
            device_id=line[dz], device_id_type=MESH).wait_recv()
    total = zbuf[0]
    for n in range(1, NZ):
        total += zbuf[n]
    final[mine] = total

    acopies = []
    for n, (where, _) in enumerate(plane):
        copy = pltpu.make_async_remote_copy(
            src_ref=final.at[mine], dst_ref=final.at[mine], send_sem=ag_send.at[n], recv_sem=ag_recv.at[mine],
            device_id=where, device_id_type=MESH)
        copy.start()
        acopies.append(copy)
    for where, piece in plane:
        pltpu.make_async_remote_copy(
            src_ref=final.at[piece], dst_ref=final.at[piece], send_sem=ag_send.at[0], recv_sem=ag_recv.at[piece],
            device_id=where, device_id_type=MESH).wait_recv()
    out[...] = final[...]
    for copy in copies + zcopies + acopies:
        copy.wait_send()


def summed_gram(matrix, pattern, chunks=4):
    rows = matrix.shape[0]
    piece = (PIECE, BLOCK)
    dma = pltpu.SemaphoreType.DMA
    hbm = pl.BlockSpec(memory_space=pltpu.HBM)
    vmem = pl.BlockSpec(memory_space=pltpu.VMEM)
    return pl.pallas_call(
        functools.partial(gram_kernel, chunks),
        out_shape=(jax.ShapeDtypeStruct((PLANE,) + piece, F32), jax.ShapeDtypeStruct((rows, NB), BF16)),
        in_specs=[hbm, hbm],
        out_specs=(vmem, vmem),
        scratch_shapes=[
            pltpu.SMEM(pattern.shape, jnp.int32),
            pltpu.VMEM((PLANE,) + piece, F32),
            pltpu.VMEM((PLANE - 1,) + piece, F32),
            pltpu.VMEM((NZ,) + piece, F32),
            pltpu.VMEM((PLANE,) + piece, F32),
            dma((chunks,)), dma,
            dma((PLANE - 1,)), dma((PLANE - 1,)),
            dma((NZ - 1,)), dma((NZ,)),
            dma((PLANE - 1,)), dma((PLANE,)),
            pltpu.SemaphoreType.REGULAR,
        ],
        compiler_params=pltpu.CompilerParams(collective_id=0, has_side_effects=True, vmem_limit_bytes=24 << 20),
        cost_estimate=pl.CostEstimate(flops=2 * rows * NB * NB, bytes_accessed=2 * rows * NB, transcendentals=0),
        name="gram_sum",
    )(matrix, pattern)


def eliminate(panel, at, size, group, tick):
    tiles, lanes = size // 8, panel.shape[1] // 128
    tile = (8, 128)
    parts = [[panel[8 * t : 8 * t + 8, 128 * c : 128 * c + 128] for c in range(lanes)] for t in range(tiles)]
    sub = lax.broadcasted_iota(jnp.int32, tile, 0)
    pivots = [None] * tiles
    for q in range(0, size, group):
        cols = []
        for k in range(q, q + group):
            c, lane = divmod(at + k, 128)
            cols.append([
                jnp.broadcast_to(parts[t][c][:, lane : lane + 1], tile) if t >= k // 8 else None for t in range(tiles)
            ])
        for j in range(q, q + group):
            t0, s = divmod(j, 8)
            col = cols[j - q]
            pivot = jnp.broadcast_to(col[t0][s : s + 1], tile)
            inverse = 1.0 / pivot
            pivots[t0] = pivot if s == 0 else jnp.where(sub >= s, pivot, pivots[t0])
            scaled = [col[t] * inverse if t >= t0 else None for t in range(tiles)]
            for k in range(j + 1, q + group):
                tk, sk = divmod(k, 8)
                row = jnp.broadcast_to(col[tk][sk : sk + 1], tile)
                for t in range(tk, tiles):
                    term = (col[t] * row) * inverse if k == j + 1 else scaled[t] * row
                    cols[k - q][t] = cols[k - q][t] - term
            heads = [jnp.broadcast_to(parts[t0][c][s : s + 1], tile) for c in range(lanes)]
            for t in range(t0, tiles):
                if t == t0 and s == 7:
                    continue
                factors = jnp.where(sub > s, scaled[t], 0.0) if t == t0 else scaled[t]
                for c in range(lanes):
                    parts[t][c] = parts[t][c] - factors * heads[c]
            tick()
    rows = []
    for t in range(tiles):
        scale = lax.rsqrt(pivots[t])
        rows.append(jnp.concatenate([p * scale for p in parts[t]], axis=1))
    return jnp.concatenate(rows, axis=0)


def split(value, terms):
    parts = []
    for _ in range(terms):
        parts.append(value.astype(BF16))
        value = value - parts[-1].astype(F32)
    return parts


def factor(work, size, group, done, tick):
    n = work.shape[0]
    for r0 in range(0, n, size):
        r1 = r0 + size
        low, high = r0 // 128 * 128, n + (r1 + 127) // 128 * 128
        rows = eliminate(work[r0:r1, low:high], r0 - low, size, group, tick)
        work[r0:r1, low:high] = rows
        cut = r1 // 128 * 128
        if r1 < n:
            h, m, l = split(rows, 3)
            left = jnp.concatenate([h, h, m, h, l, m], axis=0)
            right = jnp.concatenate([h, m, h, l, h, m], axis=0)[:, cut - low :]
            for a, e in ((r1, r1 + size), (r1 + size, n)):
                if a < e:
                    work[a:e, cut:high] = work[a:e, cut:high] - lax.dot_general(
                        left[:, a - low : e - low], right, (((0,), (0,)), ((), ())), preferred_element_type=F32)
        done(r1)


def basis_kernel(total_rows, gram, masked, basis, upper, work, triangle, made, out_sems, upper_sem):
    rows = masked.shape[0]
    pieces, chunks = rows // BLOCK, out_sems.shape[1]
    step = rows // chunks

    scale = 1.0 / total_rows
    g01 = gram[: PLANE // 2, :8, :].reshape(BLOCK, BLOCK) * scale
    both = gram[PLANE // 2 :, :8, :].reshape(BLOCK, BLOCK) * scale
    diagonal = gram[0, 8:, :] * scale
    flipped = both.T
    r = lax.broadcasted_iota(jnp.int32, (BLOCK, BLOCK), 0)
    c = lax.broadcasted_iota(jnp.int32, (BLOCK, BLOCK), 1)
    unit = jnp.where(r == c, 1.0, 0.0)
    zero = jnp.zeros((BLOCK, BLOCK), F32)
    work[:BLOCK, :BLOCK] = jnp.where(c >= r, both, flipped)
    work[:BLOCK, BLOCK:NB] = g01
    work[BLOCK:, BLOCK:NB] = jnp.where(c < r, both, jnp.where(c > r, flipped, diagonal))
    work[:BLOCK, NB : NB + BLOCK] = unit
    work[:BLOCK, NB + BLOCK :] = zero
    work[BLOCK:, NB : NB + BLOCK] = zero
    work[BLOCK:, NB + BLOCK :] = unit

    stores = []

    def send_out(i, half):
        part = (pl.ds(i * step, step), pl.ds(half * BLOCK, BLOCK))
        store = pltpu.make_async_copy(made.at[part], basis.at[part], out_sems.at[half, i])
        store.start()
        stores.append(store)

    state = {"weights": None, "ticks": 0, "next": 0}

    def first_half(i):
        rows_i = pl.ds(i * BLOCK, BLOCK)
        left = masked[rows_i, :BLOCK]
        product = jnp.dot(jnp.concatenate([left, left], axis=1), state["weights"], preferred_element_type=F32)
        made[rows_i, :BLOCK] = product.astype(BF16)
        if (i + 1) * BLOCK % step == 0:
            send_out((i + 1) * BLOCK // step - 1, 0)

    def tick():
        if state["weights"] is not None:
            state["ticks"] += 1
            while state["next"] < min(pieces, state["ticks"] * pieces // (NB - BLOCK)):
                first_half(state["next"])
                state["next"] += 1

    def done(count):
        if count == BLOCK:
            corner = jnp.where(c <= r, work[:BLOCK, NB : NB + BLOCK], 0.0).T
            state["weights"] = jnp.concatenate(split(corner, 2), axis=0)

    factor(work, 32, 16, done, tick)

    triangle[:BLOCK, :BLOCK] = jnp.where(c >= r, work[:BLOCK, :BLOCK], 0.0)
    triangle[:BLOCK, BLOCK:] = work[:BLOCK, BLOCK:NB]
    triangle[BLOCK:, :BLOCK] = zero
    triangle[BLOCK:, BLOCK:] = jnp.where(c >= r, work[BLOCK:, BLOCK:NB], 0.0)
    upper_store = pltpu.make_async_copy(triangle, upper, upper_sem)
    upper_store.start()
    stores.append(upper_store)

    corner = jnp.where(c <= r, work[BLOCK:, NB + BLOCK :], 0.0)
    columns = jnp.concatenate([work[BLOCK:, NB : NB + BLOCK].T, corner.T], axis=0)
    weights = jnp.concatenate(split(columns, 2), axis=1)
    for i in range(chunks):
        part = pl.ds(i * step, step)
        product = jnp.dot(masked[part, :], weights, preferred_element_type=F32)
        made[part, BLOCK:] = (product[:, :BLOCK] + product[:, BLOCK:]).astype(BF16)
        send_out(i, 1)
    for store in stores:
        store.wait()


def factor_and_basis(gram, masked, total_rows, chunks=8):
    rows = masked.shape[0]
    vmem = pl.BlockSpec(memory_space=pltpu.VMEM)
    hbm = pl.BlockSpec(memory_space=pltpu.HBM)
    return pl.pallas_call(
        functools.partial(basis_kernel, float(total_rows)),
        out_shape=(jax.ShapeDtypeStruct((rows, NB), BF16), jax.ShapeDtypeStruct((NB, NB), F32)),
        in_specs=[vmem, vmem],
        out_specs=(hbm, hbm),
        scratch_shapes=[
            pltpu.VMEM((NB, 2 * NB), F32),
            pltpu.VMEM((NB, NB), F32),
            pltpu.VMEM((rows, NB), BF16),
            pltpu.SemaphoreType.DMA((2, chunks)),
            pltpu.SemaphoreType.DMA,
        ],
        compiler_params=pltpu.CompilerParams(vmem_limit_bytes=24 << 20),
        cost_estimate=pl.CostEstimate(flops=4 * rows * NB * NB, bytes_accessed=4 * rows * NB, transcendentals=0),
        name="factor_basis",
    )(gram, masked)


def local(matrix, pattern):
    total_rows = matrix.shape[0] * lax.axis_size("gx") * lax.axis_size("gy")
    gram, masked = summed_gram(pltpu.with_memory_space_constraint(matrix, pltpu.HBM), pltpu.with_memory_space_constraint(pattern.T, pltpu.HBM))
    return factor_and_basis(gram, masked, total_rows)


def solution(mesh):
    placed = (P(("gx", "gy"), None), P(("gx", "gy"), None))
    return jax.shard_map(
        local, mesh=mesh, in_specs=placed, out_specs=(P(("gx", "gy"), None), P()), check_vma=False
    )
```

time: 52.9 us -> 43.5 us (0.82)
  Pallas kernels: 49.7 us -> 42.7 us
  local copies, waits for them, and re-layouts: 2.35 us -> 0 us
    pallas_call x2, Pallas kernels: 49.7 us -> 42.7 us  [the longest x1 34.6 us: summed_gram(): pl.pallas_call(functools.partial(gram_kernel, chunks), out_shape=(jax.Sha...]
    unnamed x3 -> x0, local copies, waits for them, and re-layouts: 2.35 us -> none
where the time goes in v2:
time: 43.5 us; the launch traced here: 43.3 us
  Pallas kernels  42.7 us (98%)
  between operations  0.64 us (1%)
    pallas_call x1, Pallas kernels, summed_gram(): pl.pallas_call(functools.partial(gram_kernel, chunks), out_shape=(jax.Sha...  34.6 us
    pallas_call x1, Pallas kernels, factor_and_basis(): pl.pallas_call(functools.partial(basis_kernel, float(total_rows)), out_sh...  8.15 us

profile of v2, /device:TPU:1, one launch (start us, length us, event | category | flops | bytes accessed | tf_op | source)
XLA Modules:
  0.0 43.3 jit_solution(5097517143065272674)
XLA Ops:
  0.6 34.6 %gram_sum.1 = (f32[32,9,128]{2,1,0:T(8,128)S(1)}, bf16[4096,256]{1,0:T(8,128)(2,1)S(1)}) custom-call(bf16[4096,256]{1,0:T(8,128)(2,1)} %matrix.1, s32[2,32]{1,0:T(2,128)} %bitcast.1), custom_call_target="tpu_custom_call" | custom-call | flops 536870912 | bytes 2097152 | tf_op jit(solution)/shard_map/gram_sum/pallas_call | solution.py:148
  35.2 8.2 %factor_basis.1 = (bf16[4096,256]{1,0:T(8,128)(2,1)}, f32[256,256]{1,0:T(8,128)}) custom-call(f32[32,9,128]{2,1,0:T(8,128)S(1)} %get-tuple-element.4.gram, bf16[4096,256]{1,0:T(8,128)(2,1)S(1)} %get-tuple-element.5.masked), custom_call_target="tpu_custom_call" | custom-call | flops 1073741824 | bytes 4194304 | tf_op jit(solution)/shard_map/factor_basis/pallas_call | solution.py:317

commit v3 on v2

--- a/solution.py
+++ b/solution.py
@@ -15,19 +15,29 @@
 
 NX, NY, NZ, NC = 4, 4, 16, 2
 PLANE = NX * NY * NC
-PIECE = 9
+OWNERS = ((0, 0), (1, 0), (2, 0), (3, 0), (0, 1), (0, 2), (0, 3), (1, 1))
+PIECES = len(OWNERS) * NC
+PIECE = NB // PIECES + 1
+PASSED = ((), tuple(range(15, 9, -1)), tuple(range(3, 10)))
+NEAR = len(PASSED)
 
 
 def ring(step, size):
     return min(step, size - step)
 
 
+def sender_order(chip):
+    return -(ring(3 - chip[0], NX) + ring(3 - chip[1], NY))
+
+
+PIECE_ORDER = [n * NC + core for n in sorted(range(len(OWNERS)), key=lambda n: sender_order(OWNERS[n])) for core in range(NC)]
+PLANE_ORDER = sorted(
+    ((x, y, core) for x in range(NX) for y in range(NY) for core in range(NC)), key=lambda s: (s[0] + s[1], s[0], s[1])
+)
 PLANE_STEPS = sorted(
     ((dx, dy, dc) for dx in range(NX) for dy in range(NY) for dc in range(NC) if dx or dy or dc),
     key=lambda s: -(ring(s[0], NX) + ring(s[1], NY) + 0.5 * s[2]),
 )
-Z_STEPS = sorted(range(1, NZ), key=lambda s: -ring(s, NZ))
-Z_NEAR = [s for s in Z_STEPS if ring(s, NZ) <= 4]
 
 
 def place():
@@ -41,22 +51,36 @@
 
 
 def gram_kernel(chunks, matrix, pattern, out, masked, keeps, send, recv, zbuf, final,
-                in_sems, keep_sem, rs_send, rs_recv, z_send, z_recv, ag_send, ag_recv, far_sem):
+                in_sems, keep_sem, rs_send, rs_recv, z_send, z_recv, pass_send, pass_recv, ag_send, ag_recv):
     rows = masked.shape[0]
     step = rows // chunks
     x, y, z, core = place()
     mine = (x * NY + y) * NC + core
-    plane = []
-    for dx, dy, dc in PLANE_STEPS:
-        px, py, pc = (x + dx) % NX, (y + dy) % NY, (core + dc) % NC
-        plane.append((device(px, py, z, pc), (px * NY + py) * NC + pc))
-    line = {dz: device(x, y, (z + dz) % NZ, core) for dz in Z_STEPS}
+    some_x, some_y = (x + NX - 1) // NX, (y + NY - 1) // NY
+    both_one = ((NX - x) // 3) * ((NY - y) // 3)
+    owner = 1 - some_x * some_y * (1 - both_one)
+    piece = ((1 - some_y) * x + some_y * (3 + y + 3 * some_x)) * NC + core
+    near = 1 - (z + NZ - NEAR) // NZ
+
+    def owner_of(n):
+        return OWNERS[n // NC] + (n % NC,)
+
+    def number(spot):
+        return (spot[0] * NY + spot[1]) * NC + spot[2]
 
     barrier = pltpu.get_barrier_semaphore()
-    for where, _ in plane:
-        pl.semaphore_signal(barrier, inc=1, device_id=where, device_id_type=MESH)
-    for dz in Z_NEAR:
-        pl.semaphore_signal(barrier, inc=1, device_id=line[dz], device_id_type=MESH)
+
+    @pl.when(owner == 1)
+    def _():
+        for dx, dy, dc in PLANE_STEPS:
+            where = device((x + dx) % NX, (y + dy) % NY, z, (core + dc) % NC)
+            pl.semaphore_signal(barrier, inc=1, device_id=where, device_id_type=MESH)
+
+    @pl.when(owner * near == 1)
+    def _():
+        for dz in range(1, NZ):
+            where = device(x, y, (z + dz) % NZ, core)
+            pl.semaphore_signal(barrier, inc=1, device_id=where, device_id_type=MESH)
 
     keep_load = pltpu.make_async_copy(pattern, keeps, keep_sem)
     keep_load.start()
@@ -68,7 +92,8 @@
         loads.append(load)
 
     keep_load.wait()
-    gram = jnp.zeros((NB, NB), F32)
+    top, corner = jnp.zeros((BLOCK, NB), F32), jnp.zeros((BLOCK, BLOCK), F32)
+    dims = (((0,), (0,)), ((), ()))
     for i in range(chunks):
         loads[i].wait()
         for at in range(i * step, i * step + step, BLOCK):
@@ -76,91 +101,125 @@
                 block = (slice(at, at + BLOCK), slice(h * BLOCK, h * BLOCK + BLOCK))
                 masked[block] = jnp.where(keeps[h, at // BLOCK] != 0, masked[block], 0).astype(BF16)
         part = masked[i * step : i * step + step, :]
-        gram += lax.dot_general(part, part, (((0,), (0,)), ((), ())), preferred_element_type=F32)
+        top += lax.dot_general(part[:, :BLOCK], part, dims, preferred_element_type=F32)
+        corner += lax.dot_general(part[:, BLOCK:], part[:, BLOCK:], dims, preferred_element_type=F32)
 
     r = lax.broadcasted_iota(jnp.int32, (BLOCK, BLOCK), 0)
     c = lax.broadcasted_iota(jnp.int32, (BLOCK, BLOCK), 1)
-    g00, g01, g11 = gram[:BLOCK, :BLOCK], gram[:BLOCK, BLOCK:], gram[BLOCK:, BLOCK:]
-    both = jnp.where(c >= r, g00, g11)
-    diagonal = jnp.sum(jnp.where(c == r, g11, 0.0), axis=0, keepdims=True)
-    send[: PLANE // 2, :8, :] = g01.reshape(PLANE // 2, 8, BLOCK)
-    send[PLANE // 2 :, :8, :] = both.reshape(PLANE // 2, 8, BLOCK)
-    send[:, 8:, :] = jnp.broadcast_to(diagonal[None], (PLANE, 1, BLOCK))
-
-    pl.semaphore_wait(barrier, len(plane) + len(Z_NEAR))
-
-    copies = []
-    for n, (where, piece) in enumerate(plane):
-        copy = pltpu.make_async_remote_copy(
-            src_ref=send.at[piece], dst_ref=recv.at[n], send_sem=rs_send.at[n], recv_sem=rs_recv.at[n],
-            device_id=where, device_id_type=MESH)
-        copy.start()
-        copies.append(copy)
-    for dz in (4, NZ - 4):
-        pl.semaphore_signal(far_sem, inc=1, device_id=line[dz], device_id_type=MESH)
-    for copy in copies:
-        copy.wait_recv()
-    total = send[mine]
-    for n in range(len(plane)):
-        total += recv[n]
-    zbuf[z] = total
-    pl.semaphore_wait(far_sem, 2)
-
-    zcopies = []
-    for n, dz in enumerate(Z_STEPS):
-        copy = pltpu.make_async_remote_copy(
-            src_ref=zbuf.at[z], dst_ref=zbuf.at[z], send_sem=z_send.at[n], recv_sem=z_recv.at[z],
-            device_id=line[dz], device_id_type=MESH)
-        copy.start()
-        zcopies.append(copy)
-    for dz in Z_STEPS:
-        other = (z + dz) % NZ
-        pltpu.make_async_remote_copy(
-            src_ref=zbuf.at[other], dst_ref=zbuf.at[other], send_sem=z_send.at[0], recv_sem=z_recv.at[other],
-            device_id=line[dz], device_id_type=MESH).wait_recv()
-    total = zbuf[0]
-    for n in range(1, NZ):
-        total += zbuf[n]
-    final[mine] = total
-
-    acopies = []
-    for n, (where, _) in enumerate(plane):
-        copy = pltpu.make_async_remote_copy(
-            src_ref=final.at[mine], dst_ref=final.at[mine], send_sem=ag_send.at[n], recv_sem=ag_recv.at[mine],
-            device_id=where, device_id_type=MESH)
-        copy.start()
-        acopies.append(copy)
-    for where, piece in plane:
-        pltpu.make_async_remote_copy(
-            src_ref=final.at[piece], dst_ref=final.at[piece], send_sem=ag_send.at[0], recv_sem=ag_recv.at[piece],
-            device_id=where, device_id_type=MESH).wait_recv()
+    both = jnp.where(c >= r, top[:, :BLOCK], corner)
+    diagonal = jnp.sum(jnp.where(c == r, corner, 0.0), axis=0, keepdims=True)
+    send[: PIECES // 2, : PIECE - 1, :] = top[:, BLOCK:].reshape(PIECES // 2, PIECE - 1, BLOCK)
+    send[PIECES // 2 :, : PIECE - 1, :] = both.reshape(PIECES // 2, PIECE - 1, BLOCK)
+    send[:, PIECE - 1 :, :] = jnp.broadcast_to(diagonal[None], (PIECES, 1, BLOCK))
+
+    pl.semaphore_wait(barrier, PIECES + owner * (NEAR - 1 - near))
+
+    def to_owner(n):
+        spot = owner_of(n)
+        return pltpu.make_async_remote_copy(
+            src_ref=send.at[n], dst_ref=recv.at[mine], send_sem=rs_send.at[n], recv_sem=rs_recv.at[mine],
+            device_id=device(spot[0], spot[1], z, spot[2]), device_id_type=MESH)
+
+    for n in PIECE_ORDER:
+        pl.when(mine != number(owner_of(n)))(to_owner(n).start)
+
+    def along_z(other, to):
+        return pltpu.make_async_remote_copy(
+            src_ref=zbuf.at[other], dst_ref=zbuf.at[other], send_sem=z_send.at[to], recv_sem=z_recv.at[other],
+            device_id=device(x, y, to, core), device_id_type=MESH)
+
+    def passed(to):
+        return pltpu.make_async_remote_copy(
+            src_ref=final.at[piece], dst_ref=final.at[piece], send_sem=pass_send.at[to], recv_sem=pass_recv,
+            device_id=device(x, y, to, core), device_id_type=MESH)
+
+    def gathered(n, spot):
+        return pltpu.make_async_remote_copy(
+            src_ref=final.at[n], dst_ref=final.at[n], send_sem=ag_send.at[number(spot)], recv_sem=ag_recv.at[n],
+            device_id=device(spot[0], spot[1], z, spot[2]), device_id_type=MESH)
+
+    @pl.when(owner == 1)
+    def _():
+        others = []
+        for dx, dy, dc in PLANE_STEPS:
+            others.append((((x + dx) % NX) * NY + (y + dy) % NY) * NC + (core + dc) % NC)
+        for other in others:
+            pltpu.make_async_remote_copy(
+                src_ref=send.at[piece], dst_ref=recv.at[other], send_sem=rs_send.at[0], recv_sem=rs_recv.at[other],
+                device_id=device(x, y, z, 1 - core), device_id_type=MESH).wait_recv()
+        total = send[piece]
+        for other in others:
+            total += recv[other]
+        zbuf[z] = total
+        for to in range(NEAR):
+            pl.when(z != to)(along_z(z, to).start)
+
+        @pl.when(near == 1)
+        def _():
+            for dz in range(1, NZ):
+                along_z((z + dz) % NZ, 0).wait_recv()
+            total = zbuf[0]
+            for n in range(1, NZ):
+                total += zbuf[n]
+            final[piece] = total
+            for at in range(NEAR):
+                if PASSED[at]:
+                    @pl.when(z == at)
+                    def _():
+                        for to in PASSED[at]:
+                            passed(to).start()
+
+        @pl.when(near == 0)
+        def _():
+            passed(0).wait_recv()
+
+        for spot in PLANE_ORDER:
+            pl.when(mine != number(spot))(gathered(piece, spot).start)
+
+    for n in range(PIECES):
+        spot = owner_of(n)
+        pl.when(mine != number(spot))(gathered(n, spot).wait_recv)
     out[...] = final[...]
-    for copy in copies + zcopies + acopies:
-        copy.wait_send()
-
-
-def summed_gram(matrix, pattern, chunks=4):
+
+    for n in range(PIECES):
+        pl.when(mine != number(owner_of(n)))(to_owner(n).wait_send)
+
+    @pl.when(owner == 1)
+    def _():
+        for to in range(NEAR):
+            pl.when(z != to)(along_z(z, to).wait_send)
+        for at in range(NEAR):
+            if PASSED[at]:
+                @pl.when(z == at)
+                def _():
+                    for to in PASSED[at]:
+                        passed(to).wait_send()
+        for spot in PLANE_ORDER:
+            pl.when(mine != number(spot))(gathered(piece, spot).wait_send)
+
+
+def summed_gram(matrix, pattern, chunks=2):
     rows = matrix.shape[0]
-    piece = (PIECE, BLOCK)
+    part = (PIECE, BLOCK)
     dma = pltpu.SemaphoreType.DMA
     hbm = pl.BlockSpec(memory_space=pltpu.HBM)
     vmem = pl.BlockSpec(memory_space=pltpu.VMEM)
     return pl.pallas_call(
         functools.partial(gram_kernel, chunks),
-        out_shape=(jax.ShapeDtypeStruct((PLANE,) + piece, F32), jax.ShapeDtypeStruct((rows, NB), BF16)),
+        out_shape=(jax.ShapeDtypeStruct((PIECES,) + part, F32), jax.ShapeDtypeStruct((rows, NB), BF16)),
         in_specs=[hbm, hbm],
         out_specs=(vmem, vmem),
         scratch_shapes=[
             pltpu.SMEM(pattern.shape, jnp.int32),
-            pltpu.VMEM((PLANE,) + piece, F32),
-            pltpu.VMEM((PLANE - 1,) + piece, F32),
-            pltpu.VMEM((NZ,) + piece, F32),
-            pltpu.VMEM((PLANE,) + piece, F32),
+            pltpu.VMEM((PIECES,) + part, F32),
+            pltpu.VMEM((PLANE,) + part, F32),
+            pltpu.VMEM((NZ,) + part, F32),
+            pltpu.VMEM((PIECES,) + part, F32),
             dma((chunks,)), dma,
-            dma((PLANE - 1,)), dma((PLANE - 1,)),
-            dma((NZ - 1,)), dma((NZ,)),
-            dma((PLANE - 1,)), dma((PLANE,)),
-            pltpu.SemaphoreType.REGULAR,
+            dma((PIECES,)), dma((PLANE,)),
+            dma((NEAR,)), dma((NZ,)),
+            dma((NZ,)), dma,
+            dma((PLANE,)), dma((PIECES,)),
         ],
         compiler_params=pltpu.CompilerParams(collective_id=0, has_side_effects=True, vmem_limit_bytes=24 << 20),
         cost_estimate=pl.CostEstimate(flops=2 * rows * NB * NB, bytes_accessed=2 * rows * NB, transcendentals=0),
@@ -242,9 +301,9 @@
     step = rows // chunks
 
     scale = 1.0 / total_rows
-    g01 = gram[: PLANE // 2, :8, :].reshape(BLOCK, BLOCK) * scale
-    both = gram[PLANE // 2 :, :8, :].reshape(BLOCK, BLOCK) * scale
-    diagonal = gram[0, 8:, :] * scale
+    g01 = gram[: PIECES // 2, : PIECE - 1, :].reshape(BLOCK, BLOCK) * scale
+    both = gram[PIECES // 2 :, : PIECE - 1, :].reshape(BLOCK, BLOCK) * scale
+    diagonal = gram[0, PIECE - 1 :, :] * scale
     flipped = both.T
     r = lax.broadcasted_iota(jnp.int32, (BLOCK, BLOCK), 0)
     c = lax.broadcasted_iota(jnp.int32, (BLOCK, BLOCK), 1)

time: 43.5 us -> 42.2 us (0.970)
  Pallas kernels: 42.7 us -> 41.4 us
    pallas_call x1, Pallas kernels: 34.6 us -> 33.2 us  [summed_gram(): pl.pallas_call(functools.partial(gram_kernel, chunks), out_shape=(jax.Sha...]
where the time goes in v3:
time: 42.2 us; the launch traced here: 42 us
  Pallas kernels  41.4 us (98%)
  between operations  0.64 us (2%)
    pallas_call x1, Pallas kernels, summed_gram(): pl.pallas_call(functools.partial(gram_kernel, chunks), out_shape=(jax.Sha...  33.2 us
    pallas_call x1, Pallas kernels, factor_and_basis(): pl.pallas_call(functools.partial(basis_kernel, float(total_rows)), out_sh...  8.15 us

profile of v3, /device:TPU:1, one launch (start us, length us, event | category | flops | bytes accessed | tf_op | source)
XLA Modules:
  0.0 42.0 jit_solution(5952081455415997047)
XLA Ops:
  0.6 33.2 %gram_sum.1 = (f32[16,17,128]{2,1,0:T(8,128)S(1)}, bf16[4096,256]{1,0:T(8,128)(2,1)S(1)}) custom-call(bf16[4096,256]{1,0:T(8,128)(2,1)} %matrix.1, s32[2,32]{1,0:T(2,128)} %bitcast.1), custom_call_target="tpu_custom_call" | custom-call | flops 536870912 | bytes 2097152 | tf_op jit(solution)/shard_map/gram_sum/pallas_call | solution.py:207
  33.9 8.2 %factor_basis.1 = (bf16[4096,256]{1,0:T(8,128)(2,1)}, f32[256,256]{1,0:T(8,128)}) custom-call(f32[16,17,128]{2,1,0:T(8,128)S(1)} %get-tuple-element.4.gram, bf16[4096,256]{1,0:T(8,128)(2,1)S(1)} %get-tuple-element.5.masked), custom_call_target="tpu_custom_call" | custom-call | flops 1073741824 | bytes 4194304 | tf_op jit(solution)/shard_map/factor_basis/pallas_call | solution.py:376

commit v4 on v3

--- a/solution.py
+++ b/solution.py
@@ -42,25 +42,31 @@
 
 def place():
     gx, gy = lax.axis_index("gx"), lax.axis_index("gy")
-    x = gx // (NY * NC) * 2 + gy // NZ
-    return x, gx // NC % NY, gy % NZ, gx % NC
-
-
-def device(x, y, z, core):
-    return (x // 2 * NY + y) * NC + core, x % 2 * NZ + z
-
-
-def gram_kernel(chunks, matrix, pattern, out, masked, keeps, send, recv, zbuf, final,
+    x = 2 * lax.div(gx, NY * NC) + lax.div(gy, NZ)
+    return x, lax.rem(lax.div(gx, NC), NY), lax.rem(gy, NZ), lax.rem(gx, NC)
+
+
+def gram_kernel(cuts, matrix, pattern, out, masked, keeps, send, recv, zbuf, final,
                 in_sems, keep_sem, rs_send, rs_recv, z_send, z_recv, pass_send, pass_recv, ag_send, ag_recv):
-    rows = masked.shape[0]
-    step = rows // chunks
+    loads = []
+    at = 0
+    for i, rows in enumerate(cuts):
+        part = pl.ds(at, rows)
+        load = pltpu.make_async_copy(matrix.at[part], masked.at[part], in_sems.at[i])
+        load.start()
+        loads.append(load)
+        at += rows
+    keep_load = pltpu.make_async_copy(pattern, keeps, keep_sem)
+    keep_load.start()
+
     x, y, z, core = place()
+    gx, gy = lax.axis_index("gx"), lax.axis_index("gy")
     mine = (x * NY + y) * NC + core
-    some_x, some_y = (x + NX - 1) // NX, (y + NY - 1) // NY
-    both_one = ((NX - x) // 3) * ((NY - y) // 3)
+    some_x, some_y = lax.div(x + NX - 1, NX), lax.div(y + NY - 1, NY)
+    both_one = lax.div(NX - x, 3) * lax.div(NY - y, 3)
     owner = 1 - some_x * some_y * (1 - both_one)
     piece = ((1 - some_y) * x + some_y * (3 + y + 3 * some_x)) * NC + core
-    near = 1 - (z + NZ - NEAR) // NZ
+    near = 1 - lax.div(z + NZ - NEAR, NZ)
 
     def owner_of(n):
         return OWNERS[n // NC] + (n % NC,)
@@ -68,41 +74,44 @@
     def number(spot):
         return (spot[0] * NY + spot[1]) * NC + spot[2]
 
+    def spot_id(spot):
+        return (spot[0] // 2 * NY + spot[1]) * NC + spot[2], spot[0] % 2 * NZ + z
+
+    def plane_id(to):
+        return gx, gy - z + to
+
     barrier = pltpu.get_barrier_semaphore()
 
     @pl.when(owner == 1)
     def _():
+        at_x = [lax.rem(x + d, NX) for d in range(NX)]
+        at_y = [lax.rem(y + d, NY) * NC for d in range(NY)]
+        at_core = [core, 1 - core]
+        high = [lax.div(v, 2) * (NY * NC) for v in at_x]
+        low = [lax.rem(v, 2) * NZ + z for v in at_x]
         for dx, dy, dc in PLANE_STEPS:
-            where = device((x + dx) % NX, (y + dy) % NY, z, (core + dc) % NC)
-            pl.semaphore_signal(barrier, inc=1, device_id=where, device_id_type=MESH)
+            pl.semaphore_signal(
+                barrier, inc=1, device_id=(high[dx] + at_y[dy] + at_core[dc], low[dx]), device_id_type=MESH)
 
     @pl.when(owner * near == 1)
     def _():
         for dz in range(1, NZ):
-            where = device(x, y, (z + dz) % NZ, core)
-            pl.semaphore_signal(barrier, inc=1, device_id=where, device_id_type=MESH)
-
-    keep_load = pltpu.make_async_copy(pattern, keeps, keep_sem)
-    keep_load.start()
-    loads = []
-    for i in range(chunks):
-        part = pl.ds(i * step, step)
-        load = pltpu.make_async_copy(matrix.at[part], masked.at[part], in_sems.at[i])
-        load.start()
-        loads.append(load)
+            pl.semaphore_signal(barrier, inc=1, device_id=plane_id(lax.rem(z + dz, NZ)), device_id_type=MESH)
 
     keep_load.wait()
     top, corner = jnp.zeros((BLOCK, NB), F32), jnp.zeros((BLOCK, BLOCK), F32)
     dims = (((0,), (0,)), ((), ()))
-    for i in range(chunks):
+    start = 0
+    for i, rows in enumerate(cuts):
         loads[i].wait()
-        for at in range(i * step, i * step + step, BLOCK):
+        for at in range(start, start + rows, BLOCK):
             for h in range(NB // BLOCK):
                 block = (slice(at, at + BLOCK), slice(h * BLOCK, h * BLOCK + BLOCK))
                 masked[block] = jnp.where(keeps[h, at // BLOCK] != 0, masked[block], 0).astype(BF16)
-        part = masked[i * step : i * step + step, :]
+        part = masked[start : start + rows, :]
         top += lax.dot_general(part[:, :BLOCK], part, dims, preferred_element_type=F32)
         corner += lax.dot_general(part[:, BLOCK:], part[:, BLOCK:], dims, preferred_element_type=F32)
+        start += rows
 
     r = lax.broadcasted_iota(jnp.int32, (BLOCK, BLOCK), 0)
     c = lax.broadcasted_iota(jnp.int32, (BLOCK, BLOCK), 1)
@@ -114,98 +123,100 @@
 
     pl.semaphore_wait(barrier, PIECES + owner * (NEAR - 1 - near))
 
+    def copy(source, target, send_sem, recv_sem, where):
+        return pltpu.make_async_remote_copy(
+            src_ref=source, dst_ref=target, send_sem=send_sem, recv_sem=recv_sem, device_id=where, device_id_type=MESH)
+
     def to_owner(n):
-        spot = owner_of(n)
-        return pltpu.make_async_remote_copy(
-            src_ref=send.at[n], dst_ref=recv.at[mine], send_sem=rs_send.at[n], recv_sem=rs_recv.at[mine],
-            device_id=device(spot[0], spot[1], z, spot[2]), device_id_type=MESH)
+        return copy(send.at[n], recv.at[mine], rs_send, rs_recv, spot_id(owner_of(n)))
+
+    def along_z(to):
+        return copy(zbuf.at[z], zbuf.at[z], z_send, z_recv, plane_id(to))
+
+    def passed(to):
+        return copy(final.at[piece], final.at[piece], pass_send, pass_recv, plane_id(to))
+
+    def gathered(spot):
+        return copy(final.at[piece], final.at[piece], ag_send, ag_recv, spot_id(spot))
+
+    def pieces(ref, count, send_sem, recv_sem):
+        part = ref.at[pl.ds(0, count)]
+        return copy(part, part, send_sem, recv_sem, spot_id((0, 0, 0)))
 
     for n in PIECE_ORDER:
         pl.when(mine != number(owner_of(n)))(to_owner(n).start)
 
-    def along_z(other, to):
-        return pltpu.make_async_remote_copy(
-            src_ref=zbuf.at[other], dst_ref=zbuf.at[other], send_sem=z_send.at[to], recv_sem=z_recv.at[other],
-            device_id=device(x, y, to, core), device_id_type=MESH)
-
-    def passed(to):
-        return pltpu.make_async_remote_copy(
-            src_ref=final.at[piece], dst_ref=final.at[piece], send_sem=pass_send.at[to], recv_sem=pass_recv,
-            device_id=device(x, y, to, core), device_id_type=MESH)
-
-    def gathered(n, spot):
-        return pltpu.make_async_remote_copy(
-            src_ref=final.at[n], dst_ref=final.at[n], send_sem=ag_send.at[number(spot)], recv_sem=ag_recv.at[n],
-            device_id=device(spot[0], spot[1], z, spot[2]), device_id_type=MESH)
+    @pl.when(owner == 0)
+    def _():
+        pieces(send, PIECES, rs_send, rs_recv).wait_send()
 
     @pl.when(owner == 1)
     def _():
-        others = []
-        for dx, dy, dc in PLANE_STEPS:
-            others.append((((x + dx) % NX) * NY + (y + dy) % NY) * NC + (core + dc) % NC)
-        for other in others:
-            pltpu.make_async_remote_copy(
-                src_ref=send.at[piece], dst_ref=recv.at[other], send_sem=rs_send.at[0], recv_sem=rs_recv.at[other],
-                device_id=device(x, y, z, 1 - core), device_id_type=MESH).wait_recv()
-        total = send[piece]
-        for other in others:
-            total += recv[other]
+        recv[mine] = send[piece]
+        pieces(recv, PLANE - 1, rs_send, rs_recv).wait_recv()
+        total = recv[0]
+        for n in range(1, PLANE):
+            total += recv[n]
         zbuf[z] = total
         for to in range(NEAR):
-            pl.when(z != to)(along_z(z, to).start)
+            pl.when(z != to)(along_z(to).start)
+        pieces(send, PIECES - 1, rs_send, rs_recv).wait_send()
 
         @pl.when(near == 1)
         def _():
-            for dz in range(1, NZ):
-                along_z((z + dz) % NZ, 0).wait_recv()
+            pieces(zbuf, NZ - 1, z_send, z_recv).wait_recv()
             total = zbuf[0]
             for n in range(1, NZ):
                 total += zbuf[n]
             final[piece] = total
-            for at in range(NEAR):
-                if PASSED[at]:
-                    @pl.when(z == at)
-                    def _():
-                        for to in PASSED[at]:
-                            passed(to).start()
 
         @pl.when(near == 0)
         def _():
-            passed(0).wait_recv()
-
-        for spot in PLANE_ORDER:
-            pl.when(mine != number(spot))(gathered(piece, spot).start)
-
-    for n in range(PIECES):
-        spot = owner_of(n)
-        pl.when(mine != number(spot))(gathered(n, spot).wait_recv)
-    out[...] = final[...]
-
-    for n in range(PIECES):
-        pl.when(mine != number(owner_of(n)))(to_owner(n).wait_send)
-
-    @pl.when(owner == 1)
-    def _():
-        for to in range(NEAR):
-            pl.when(z != to)(along_z(z, to).wait_send)
+            pieces(final, 1, pass_send, pass_recv).wait_recv()
+
         for at in range(NEAR):
             if PASSED[at]:
                 @pl.when(z == at)
                 def _():
                     for to in PASSED[at]:
-                        passed(to).wait_send()
+                        passed(to).start()
+
         for spot in PLANE_ORDER:
-            pl.when(mine != number(spot))(gathered(piece, spot).wait_send)
-
-
-def summed_gram(matrix, pattern, chunks=2):
+            pl.when(mine != number(spot))(gathered(spot).start)
+
+        @pl.when(near == 1)
+        def _():
+            pieces(zbuf, NEAR - 1, z_send, z_recv).wait_send()
+
+        @pl.when(near == 0)
+        def _():
+            pieces(zbuf, NEAR, z_send, z_recv).wait_send()
+
+        for at in range(NEAR):
+            if PASSED[at]:
+                @pl.when(z == at)
+                def _():
+                    pieces(final, len(PASSED[at]), pass_send, pass_recv).wait_send()
+
+        pieces(final, PIECES - 1, ag_send, ag_recv).wait_recv()
+        pieces(recv, PLANE - 1, ag_send, ag_recv).wait_send()
+
+    @pl.when(owner == 0)
+    def _():
+        pieces(final, PIECES, ag_send, ag_recv).wait_recv()
+
+    out[...] = final[...]
+
+
+def summed_gram(matrix, pattern):
     rows = matrix.shape[0]
+    cuts = (rows // 4, rows // 4, rows // 2)
     part = (PIECE, BLOCK)
     dma = pltpu.SemaphoreType.DMA
     hbm = pl.BlockSpec(memory_space=pltpu.HBM)
     vmem = pl.BlockSpec(memory_space=pltpu.VMEM)
     return pl.pallas_call(
-        functools.partial(gram_kernel, chunks),
+        functools.partial(gram_kernel, cuts),
         out_shape=(jax.ShapeDtypeStruct((PIECES,) + part, F32), jax.ShapeDtypeStruct((rows, NB), BF16)),
         in_specs=[hbm, hbm],
         out_specs=(vmem, vmem),
@@ -215,11 +226,8 @@
             pltpu.VMEM((PLANE,) + part, F32),
             pltpu.VMEM((NZ,) + part, F32),
             pltpu.VMEM((PIECES,) + part, F32),
-            dma((chunks,)), dma,
-            dma((PIECES,)), dma((PLANE,)),
-            dma((NEAR,)), dma((NZ,)),
-            dma((NZ,)), dma,
-            dma((PLANE,)), dma((PIECES,)),
+            dma((len(cuts),)),
+            dma, dma, dma, dma, dma, dma, dma, dma, dma,
         ],
         compiler_params=pltpu.CompilerParams(collective_id=0, has_side_effects=True, vmem_limit_bytes=24 << 20),
         cost_estimate=pl.CostEstimate(flops=2 * rows * NB * NB, bytes_accessed=2 * rows * NB, transcendentals=0),

time: 42.2 us -> 40.9 us (0.969)
  Pallas kernels: 41.4 us -> 40.1 us
    pallas_call x1, Pallas kernels: 33.2 us -> 32 us  [summed_gram(): pl.pallas_call(functools.partial(gram_kernel, cuts), out_shape=(jax.Shape...]
where the time goes in v4:
time: 40.9 us; the launch traced here: 40.8 us
  Pallas kernels  40.1 us (98%)
  between operations  0.64 us (2%)
    pallas_call x1, Pallas kernels, summed_gram(): pl.pallas_call(functools.partial(gram_kernel, cuts), out_shape=(jax.Shape...  32 us
    pallas_call x1, Pallas kernels, factor_and_basis(): pl.pallas_call(functools.partial(basis_kernel, float(total_rows)), out_sh...  8.16 us

profile of v4, /device:TPU:1, one launch (start us, length us, event | category | flops | bytes accessed | tf_op | source)
XLA Modules:
  0.0 40.8 jit_solution(1817953290361422552)
XLA Ops:
  0.6 32.0 %gram_sum.1 = (f32[16,17,128]{2,1,0:T(8,128)S(1)}, bf16[4096,256]{1,0:T(8,128)(2,1)S(1)}) custom-call(bf16[4096,256]{1,0:T(8,128)(2,1)} %matrix.1, s32[2,32]{1,0:T(2,128)} %bitcast.1), custom_call_target="tpu_custom_call" | custom-call | flops 536870912 | bytes 2097152 | tf_op jit(solution)/shard_map/gram_sum/pallas_call | solution.py:218
  32.6 8.2 %factor_basis.1 = (bf16[4096,256]{1,0:T(8,128)(2,1)}, f32[256,256]{1,0:T(8,128)}) custom-call(f32[16,17,128]{2,1,0:T(8,128)S(1)} %get-tuple-element.4.gram, bf16[4096,256]{1,0:T(8,128)(2,1)S(1)} %get-tuple-element.5.masked), custom_call_target="tpu_custom_call" | custom-call | flops 1073741824 | bytes 4194304 | tf_op jit(solution)/shard_map/factor_basis/pallas_call | solution.py:384

commit v5 on v4

--- a/solution.py
+++ b/solution.py
@@ -15,8 +15,8 @@
 
 NX, NY, NZ, NC = 4, 4, 16, 2
 PLANE = NX * NY * NC
-OWNERS = ((0, 0), (1, 0), (2, 0), (3, 0), (0, 1), (0, 2), (0, 3), (1, 1))
-PIECES = len(OWNERS) * NC
+OWNERS = tuple((x, y, 1) for x in range(NX) for y in range(NY))
+PIECES = len(OWNERS)
 PIECE = NB // PIECES + 1
 PASSED = ((), tuple(range(15, 9, -1)), tuple(range(3, 10)))
 NEAR = len(PASSED)
@@ -26,13 +26,14 @@
     return min(step, size - step)
 
 
-def sender_order(chip):
-    return -(ring(3 - chip[0], NX) + ring(3 - chip[1], NY))
-
-
-PIECE_ORDER = [n * NC + core for n in sorted(range(len(OWNERS)), key=lambda n: sender_order(OWNERS[n])) for core in range(NC)]
+def sender_order(spot):
+    return -(ring(3 - spot[0], NX) + ring(3 - spot[1], NY))
+
+
+PIECE_ORDER = sorted(range(PIECES), key=lambda n: sender_order(OWNERS[n]))
 PLANE_ORDER = sorted(
-    ((x, y, core) for x in range(NX) for y in range(NY) for core in range(NC)), key=lambda s: (s[0] + s[1], s[0], s[1])
+    ((x, y, core) for x in range(NX) for y in range(NY) for core in range(NC)),
+    key=lambda s: (s == (0, 0, 0), s[0] + s[1], s[0], s[1]),
 )
 PLANE_STEPS = sorted(
     ((dx, dy, dc) for dx in range(NX) for dy in range(NY) for dc in range(NC) if dx or dy or dc),
@@ -62,14 +63,11 @@
     x, y, z, core = place()
     gx, gy = lax.axis_index("gx"), lax.axis_index("gy")
     mine = (x * NY + y) * NC + core
-    some_x, some_y = lax.div(x + NX - 1, NX), lax.div(y + NY - 1, NY)
-    both_one = lax.div(NX - x, 3) * lax.div(NY - y, 3)
-    owner = 1 - some_x * some_y * (1 - both_one)
-    piece = ((1 - some_y) * x + some_y * (3 + y + 3 * some_x)) * NC + core
+    owner, piece = 0, 0
+    for n, (ox, oy, ocore) in enumerate(OWNERS):
+        match = (mine == (ox * NY + oy) * NC + ocore).astype(jnp.int32)
+        owner, piece = owner + match, piece + match * n
     near = 1 - lax.div(z + NZ - NEAR, NZ)
-
-    def owner_of(n):
-        return OWNERS[n // NC] + (n % NC,)
 
     def number(spot):
         return (spot[0] * NY + spot[1]) * NC + spot[2]
@@ -128,7 +126,7 @@
             src_ref=source, dst_ref=target, send_sem=send_sem, recv_sem=recv_sem, device_id=where, device_id_type=MESH)
 
     def to_owner(n):
-        return copy(send.at[n], recv.at[mine], rs_send, rs_recv, spot_id(owner_of(n)))
+        return copy(send.at[n], recv.at[mine], rs_send, rs_recv, spot_id(OWNERS[n]))
 
     def along_z(to):
         return copy(zbuf.at[z], zbuf.at[z], z_send, z_recv, plane_id(to))
@@ -144,7 +142,7 @@
         return copy(part, part, send_sem, recv_sem, spot_id((0, 0, 0)))
 
     for n in PIECE_ORDER:
-        pl.when(mine != number(owner_of(n)))(to_owner(n).start)
+        pl.when(mine != number(OWNERS[n]))(to_owner(n).start)
 
     @pl.when(owner == 0)
     def _():

time: 40.9 us -> 39.7 us (0.971)
  Pallas kernels: 40.1 us -> 38.9 us
    pallas_call x1, Pallas kernels: 32 us -> 30.7 us  [summed_gram(): pl.pallas_call(functools.partial(gram_kernel, cuts), out_shape=(jax.Shape...]
where the time goes in v5:
time: 39.7 us; the launch traced here: 39.5 us
  Pallas kernels  38.9 us (98%)
  between operations  0.64 us (2%)
    pallas_call x1, Pallas kernels, summed_gram(): pl.pallas_call(functools.partial(gram_kernel, cuts), out_shape=(jax.Shape...  30.7 us
    pallas_call x1, Pallas kernels, factor_and_basis(): pl.pallas_call(functools.partial(basis_kernel, float(total_rows)), out_sh...  8.15 us

profile of v5, /device:TPU:1, one launch (start us, length us, event | category | flops | bytes accessed | tf_op | source)
XLA Modules:
  0.0 39.5 jit_solution(13133611386884198141)
XLA Ops:
  0.6 30.7 %gram_sum.1 = (f32[16,17,128]{2,1,0:T(8,128)S(1)}, bf16[4096,256]{1,0:T(8,128)(2,1)S(1)}) custom-call(bf16[4096,256]{1,0:T(8,128)(2,1)} %matrix.1, s32[2,32]{1,0:T(2,128)} %bitcast.1), custom_call_target="tpu_custom_call" | custom-call | flops 536870912 | bytes 2097152 | tf_op jit(solution)/shard_map/gram_sum/pallas_call | solution.py:216
  31.4 8.2 %factor_basis.1 = (bf16[4096,256]{1,0:T(8,128)(2,1)}, f32[256,256]{1,0:T(8,128)}) custom-call(f32[16,17,128]{2,1,0:T(8,128)S(1)} %get-tuple-element.4.gram, bf16[4096,256]{1,0:T(8,128)(2,1)S(1)} %get-tuple-element.5.masked), custom_call_target="tpu_custom_call" | custom-call | flops 1073741824 | bytes 4194304 | tf_op jit(solution)/shard_map/factor_basis/pallas_call | solution.py:382

commit v6 on v5

--- a/solution.py
+++ b/solution.py
@@ -15,9 +15,11 @@
 
 NX, NY, NZ, NC = 4, 4, 16, 2
 PLANE = NX * NY * NC
-OWNERS = tuple((x, y, 1) for x in range(NX) for y in range(NY))
+OWNERS = tuple(
+    (x, y, 1) for x in range(NX) for y in range(NY) if (x, y) not in ((2, 2), (2, 3), (3, 2))
+)
 PIECES = len(OWNERS)
-PIECE = NB // PIECES + 1
+PIECE = -(-(NB + 1) // PIECES)
 PASSED = ((), tuple(range(15, 9, -1)), tuple(range(3, 10)))
 NEAR = len(PASSED)
 
@@ -31,10 +33,7 @@
 
 
 PIECE_ORDER = sorted(range(PIECES), key=lambda n: sender_order(OWNERS[n]))
-PLANE_ORDER = sorted(
-    ((x, y, core) for x in range(NX) for y in range(NY) for core in range(NC)),
-    key=lambda s: (s == (0, 0, 0), s[0] + s[1], s[0], s[1]),
-)
+FIRST = (0, 0, 1)
 PLANE_STEPS = sorted(
     ((dx, dy, dc) for dx in range(NX) for dy in range(NY) for dc in range(NC) if dx or dy or dc),
     key=lambda s: -(ring(s[0], NX) + ring(s[1], NY) + 0.5 * s[2]),
@@ -47,8 +46,44 @@
     return x, lax.rem(lax.div(gx, NC), NY), lax.rem(gy, NZ), lax.rem(gx, NC)
 
 
-def gram_kernel(cuts, matrix, pattern, out, masked, keeps, send, recv, zbuf, final,
+def gram_kernel(cuts, matrix, pattern, out, masked, keeps, flat, send, recv, zbuf, final,
                 in_sems, keep_sem, rs_send, rs_recv, z_send, z_recv, pass_send, pass_recv, ag_send, ag_recv):
+    x, y, z, core = place()
+    gx, gy = lax.axis_index("gx"), lax.axis_index("gy")
+    mine = (x * NY + y) * NC + core
+    owner, piece = 0, 0
+    for n, (ox, oy, ocore) in enumerate(OWNERS):
+        match = (mine == (ox * NY + oy) * NC + ocore).astype(jnp.int32)
+        owner, piece = owner + match, piece + match * n
+    near = 1 - lax.div(z + NZ - NEAR, NZ)
+
+    def number(spot):
+        return (spot[0] * NY + spot[1]) * NC + spot[2]
+
+    def spot_id(spot):
+        return (spot[0] // 2 * NY + spot[1]) * NC + spot[2], spot[0] % 2 * NZ + z
+
+    def plane_id(to):
+        return gx, gy - z + to
+
+    barrier = pltpu.get_barrier_semaphore()
+
+    @pl.when(owner == 1)
+    def _():
+        at_x = [lax.rem(x + d, NX) for d in range(NX)]
+        at_y = [lax.rem(y + d, NY) * NC for d in range(NY)]
+        at_core = [core, 1 - core]
+        high = [lax.div(v, 2) * (NY * NC) for v in at_x]
+        low = [lax.rem(v, 2) * NZ + z for v in at_x]
+        for dx, dy, dc in PLANE_STEPS:
+            pl.semaphore_signal(
+                barrier, inc=1, device_id=(high[dx] + at_y[dy] + at_core[dc], low[dx]), device_id_type=MESH)
+
+    @pl.when(owner * near == 1)
+    def _():
+        for dz in range(1, NZ):
+            pl.semaphore_signal(barrier, inc=1, device_id=plane_id(lax.rem(z + dz, NZ)), device_id_type=MESH)
+
     loads = []
     at = 0
     for i, rows in enumerate(cuts):
@@ -59,42 +94,6 @@
         at += rows
     keep_load = pltpu.make_async_copy(pattern, keeps, keep_sem)
     keep_load.start()
-
-    x, y, z, core = place()
-    gx, gy = lax.axis_index("gx"), lax.axis_index("gy")
-    mine = (x * NY + y) * NC + core
-    owner, piece = 0, 0
-    for n, (ox, oy, ocore) in enumerate(OWNERS):
-        match = (mine == (ox * NY + oy) * NC + ocore).astype(jnp.int32)
-        owner, piece = owner + match, piece + match * n
-    near = 1 - lax.div(z + NZ - NEAR, NZ)
-
-    def number(spot):
-        return (spot[0] * NY + spot[1]) * NC + spot[2]
-
-    def spot_id(spot):
-        return (spot[0] // 2 * NY + spot[1]) * NC + spot[2], spot[0] % 2 * NZ + z
-
-    def plane_id(to):
-        return gx, gy - z + to
-
-    barrier = pltpu.get_barrier_semaphore()
-
-    @pl.when(owner == 1)
-    def _():
-        at_x = [lax.rem(x + d, NX) for d in range(NX)]
-        at_y = [lax.rem(y + d, NY) * NC for d in range(NY)]
-        at_core = [core, 1 - core]
-        high = [lax.div(v, 2) * (NY * NC) for v in at_x]
-        low = [lax.rem(v, 2) * NZ + z for v in at_x]
-        for dx, dy, dc in PLANE_STEPS:
-            pl.semaphore_signal(
-                barrier, inc=1, device_id=(high[dx] + at_y[dy] + at_core[dc], low[dx]), device_id_type=MESH)
-
-    @pl.when(owner * near == 1)
-    def _():
-        for dz in range(1, NZ):
-            pl.semaphore_signal(barrier, inc=1, device_id=plane_id(lax.rem(z + dz, NZ)), device_id_type=MESH)
 
     keep_load.wait()
     top, corner = jnp.zeros((BLOCK, NB), F32), jnp.zeros((BLOCK, BLOCK), F32)
@@ -115,9 +114,11 @@
     c = lax.broadcasted_iota(jnp.int32, (BLOCK, BLOCK), 1)
     both = jnp.where(c >= r, top[:, :BLOCK], corner)
     diagonal = jnp.sum(jnp.where(c == r, corner, 0.0), axis=0, keepdims=True)
-    send[: PIECES // 2, : PIECE - 1, :] = top[:, BLOCK:].reshape(PIECES // 2, PIECE - 1, BLOCK)
-    send[PIECES // 2 :, : PIECE - 1, :] = both.reshape(PIECES // 2, PIECE - 1, BLOCK)
-    send[:, PIECE - 1 :, :] = jnp.broadcast_to(diagonal[None], (PIECES, 1, BLOCK))
+    flat[:BLOCK, :] = top[:, BLOCK:]
+    flat[BLOCK:NB, :] = both
+    flat[NB:, :] = jnp.broadcast_to(diagonal, (PIECES * PIECE - NB, BLOCK))
+    for n in range(PIECES):
+        send[n] = flat[n * PIECE : (n + 1) * PIECE, :]
 
     pl.semaphore_wait(barrier, PIECES + owner * (NEAR - 1 - near))
 
@@ -134,8 +135,8 @@
     def passed(to):
         return copy(final.at[piece], final.at[piece], pass_send, pass_recv, plane_id(to))
 
-    def gathered(spot):
-        return copy(final.at[piece], final.at[piece], ag_send, ag_recv, spot_id(spot))
+    def gathered(where):
+        return copy(final.at[piece], final.at[piece], ag_send, ag_recv, where)
 
     def pieces(ref, count, send_sem, recv_sem):
         part = ref.at[pl.ds(0, count)]
@@ -179,8 +180,14 @@
                     for to in PASSED[at]:
                         passed(to).start()
 
-        for spot in PLANE_ORDER:
-            pl.when(mine != number(spot))(gathered(spot).start)
+        pl.when(mine != number(FIRST))(gathered(spot_id(FIRST)).start)
+        at_x = [lax.rem(x + d, NX) for d in range(NX)]
+        at_y = [lax.rem(y + d, NY) for d in range(NY)]
+        at_core = [core, 1 - core]
+        for dx, dy, dc in PLANE_STEPS:
+            to = (at_x[dx], at_y[dy], at_core[dc])
+            where = (lax.div(to[0], 2) * NY + to[1]) * NC + to[2], lax.rem(to[0], 2) * NZ + z
+            pl.when(number(to) != number(FIRST))(gathered(where).start)
 
         @pl.when(near == 1)
         def _():
@@ -203,7 +210,8 @@
     def _():
         pieces(final, PIECES, ag_send, ag_recv).wait_recv()
 
-    out[...] = final[...]
+    for n in range(PIECES):
+        out[n * PIECE : (n + 1) * PIECE, :] = final[n]
 
 
 def summed_gram(matrix, pattern):
@@ -215,11 +223,12 @@
     vmem = pl.BlockSpec(memory_space=pltpu.VMEM)
     return pl.pallas_call(
         functools.partial(gram_kernel, cuts),
-        out_shape=(jax.ShapeDtypeStruct((PIECES,) + part, F32), jax.ShapeDtypeStruct((rows, NB), BF16)),
+        out_shape=(jax.ShapeDtypeStruct((PIECES * PIECE, BLOCK), F32), jax.ShapeDtypeStruct((rows, NB), BF16)),
         in_specs=[hbm, hbm],
         out_specs=(vmem, vmem),
         scratch_shapes=[
             pltpu.SMEM(pattern.shape, jnp.int32),
+            pltpu.VMEM((PIECES * PIECE, BLOCK), F32),
             pltpu.VMEM((PIECES,) + part, F32),
             pltpu.VMEM((PLANE,) + part, F32),
             pltpu.VMEM((NZ,) + part, F32),
@@ -307,9 +316,9 @@
     step = rows // chunks
 
     scale = 1.0 / total_rows
-    g01 = gram[: PIECES // 2, : PIECE - 1, :].reshape(BLOCK, BLOCK) * scale
-    both = gram[PIECES // 2 :, : PIECE - 1, :].reshape(BLOCK, BLOCK) * scale
-    diagonal = gram[0, PIECE - 1 :, :] * scale
+    g01 = gram[:BLOCK, :] * scale
+    both = gram[BLOCK:NB, :] * scale
+    diagonal = gram[NB : NB + 1, :] * scale
     flipped = both.T
     r = lax.broadcasted_iota(jnp.int32, (BLOCK, BLOCK), 0)
     c = lax.broadcasted_iota(jnp.int32, (BLOCK, BLOCK), 1)

time: 39.7 us -> 39.3 us (0.990)
  Pallas kernels: 38.9 us -> 38.5 us
where the time goes in v6:
time: 39.3 us; the launch traced here: 39.1 us
  Pallas kernels  38.5 us (98%)
  between operations  0.64 us (2%)
    pallas_call x1, Pallas kernels, summed_gram(): pl.pallas_call(functools.partial(gram_kernel, cuts), out_shape=(jax.Shape...  30.3 us
    pallas_call x1, Pallas kernels, factor_and_basis(): pl.pallas_call(functools.partial(basis_kernel, float(total_rows)), out_sh...  8.15 us

profile of v6, /device:TPU:1, one launch (start us, length us, event | category | flops | bytes accessed | tf_op | source)
XLA Modules:
  0.0 39.1 jit_solution(10660072042029266926)
XLA Ops:
  0.6 30.3 %gram_sum.1 = (f32[260,128]{1,0:T(8,128)S(1)}, bf16[4096,256]{1,0:T(8,128)(2,1)S(1)}) custom-call(bf16[4096,256]{1,0:T(8,128)(2,1)} %matrix.1, s32[2,32]{1,0:T(2,128)} %bitcast.1), custom_call_target="tpu_custom_call" | custom-call | flops 536870912 | bytes 2097152 | tf_op jit(solution)/shard_map/gram_sum/pallas_call | solution.py:224
  31.0 8.2 %factor_basis.1 = (bf16[4096,256]{1,0:T(8,128)(2,1)}, f32[256,256]{1,0:T(8,128)}) custom-call(f32[260,128]{1,0:T(8,128)S(1)} %get-tuple-element.4.gram, bf16[4096,256]{1,0:T(8,128)(2,1)S(1)} %get-tuple-element.5.masked), custom_call_target="tpu_custom_call" | custom-call | flops 1073741824 | bytes 4194304 | tf_op jit(solution)/shard_map/factor_basis/pallas_call | solution.py:391

commit v7 on v6

--- a/solution.py
+++ b/solution.py
@@ -16,7 +16,7 @@
 NX, NY, NZ, NC = 4, 4, 16, 2
 PLANE = NX * NY * NC
 OWNERS = tuple(
-    (x, y, 1) for x in range(NX) for y in range(NY) if (x, y) not in ((2, 2), (2, 3), (3, 2))
+    (x, y, 1) for x in range(NX) for y in range(NY) if x < 2 or y < 2
 )
 PIECES = len(OWNERS)
 PIECE = -(-(NB + 1) // PIECES)

time: 39.3 us -> 38.6 us (0.982)
  Pallas kernels: 38.5 us -> 37.7 us
    pallas_call x1, Pallas kernels: 30.3 us -> 29.6 us  [summed_gram(): pl.pallas_call(functools.partial(gram_kernel, cuts), out_shape=(jax.Shape...]
where the time goes in v7:
time: 38.6 us; the launch traced here: 38.4 us
  Pallas kernels  37.7 us (98%)
  between operations  0.64 us (2%)
    pallas_call x1, Pallas kernels, summed_gram(): pl.pallas_call(functools.partial(gram_kernel, cuts), out_shape=(jax.Shape...  29.6 us
    pallas_call x1, Pallas kernels, factor_and_basis(): pl.pallas_call(functools.partial(basis_kernel, float(total_rows)), out_sh...  8.15 us

profile of v7, /device:TPU:1, one launch (start us, length us, event | category | flops | bytes accessed | tf_op | source)
XLA Modules:
  0.0 38.4 jit_solution(14844807187535976387)
XLA Ops:
  0.6 29.6 %gram_sum.1 = (f32[264,128]{1,0:T(8,128)S(1)}, bf16[4096,256]{1,0:T(8,128)(2,1)S(1)}) custom-call(bf16[4096,256]{1,0:T(8,128)(2,1)} %matrix.1, s32[2,32]{1,0:T(2,128)} %bitcast.1), custom_call_target="tpu_custom_call" | custom-call | flops 536870912 | bytes 2097152 | tf_op jit(solution)/shard_map/gram_sum/pallas_call | solution.py:224
  30.2 8.2 %factor_basis.1 = (bf16[4096,256]{1,0:T(8,128)(2,1)}, f32[256,256]{1,0:T(8,128)}) custom-call(f32[264,128]{1,0:T(8,128)S(1)} %get-tuple-element.4.gram, bf16[4096,256]{1,0:T(8,128)(2,1)S(1)} %get-tuple-element.5.masked), custom_call_target="tpu_custom_call" | custom-call | flops 1073741824 | bytes 4194304 | tf_op jit(solution)/shard_map/factor_basis/pallas_call | solution.py:391
